TPU v7x, 128 devices: a whole 4x4x4 slice. The times are simulated.
128 devices in a mesh: tm: 8 (over x, core), chan: 16 (over y, z).
Axes of the slice: x: 4, y: 4, z: 4, core: 2. Of those that a mesh axis runs over, the one named last changes fastest.
Arguments:
- raw_blocks: bfloat16 [32, 10240, 1024], P('tm', 'chan'), may hold values from -6 to 6
- fir_taps: bfloat16 [128], replicated, may hold values from -0.5 to 0.5
- recorder_channel: int32 [10240], replicated, may hold values from 0 to 10239, as said below
- pairs: int32 [8192, 2], P('chan'), may hold values from 0 to 10239, as said below
Outputs:
- stacks: float32 [8192, 256], P('chan')
Inputs may be any that keep to these rules, and one draw needn't show every extreme that they name: `recorder_channel`: A permutation of the channels; each aligned block of 640 recorder rows holds exactly 40 channels of every range of 640 consecutive channels. `pairs`: each aligned block of 512 rows names exactly 32 distinct channels of every range of 640 consecutive channels.
All inputs are finite; a program needn't handle non-finite values.
Results may differ from a plain program's by a relative error of at most 0.0084.
Values may be sent and summed in bfloat16 or wider, within the bound.
A program may use at most 128 MiB of HBM per device.

v0:
```python
import jax
import jax.numpy as jnp
import numpy as np
from jax import lax
from jax.experimental import pallas as pl
from jax.experimental.pallas import tpu as pltpu
from jax.sharding import PartitionSpec as P

NB = 128
SMOOTH = 4
CAP = 64
MESH = pl.DeviceIdType.MESH
F32 = jnp.float32
BF16 = jnp.bfloat16
NT = (((1,), (1,)), ((), ()))


def table_values(length, extra):
    samples = np.arange(length, dtype=np.int64)
    freqs = np.arange(1, NB + 1, dtype=np.int64)
    angles = (samples[:, None] * freqs[None, :] % length).astype(np.float32) * np.float32(2.0 * np.pi / length)
    table = np.concatenate([np.cos(angles), -np.sin(angles)], axis=1)
    return np.concatenate([table, np.zeros((extra, 2 * NB), np.float32)]).astype(BF16)


def band_values():
    places = np.arange(NB)
    band = (np.abs(places[:, None] - places[None, :]) <= SMOOTH).astype(np.float32)
    both = np.concatenate([band, np.ones((NB, NB), np.float32)], axis=1)
    return np.concatenate([both, both]).astype(BF16)


def iota(shape, dim):
    return lax.broadcasted_iota(jnp.int32, shape, dim)


def dot(left, right):
    return jnp.dot(left, right, preferred_element_type=F32)


def dot_nt(left, right):
    return lax.dot_general(left, right, NT, preferred_element_type=F32)


def one(condition):
    return jnp.where(condition, 1.0, 0.0)


def ranks_of(marks):
    row, col = iota((128, 128), 0), iota((128, 128), 1)
    marks = jnp.where(row % 8 < 5, marks, 0.0)
    held = marks.astype(BF16)
    upto = dot(held, one(row <= col).astype(BF16))
    totals = dot(held, jnp.ones((128, 128), BF16))
    before = dot(one((row // 8 == col // 8) & (col < row)).astype(BF16), totals.astype(BF16))
    return jnp.where(marks > 0.0, upto + before - 1.0, -1.0), before


def row_of(ref, first):
    return jnp.concatenate([ref[pl.ds(first + k, 1), :] for k in range(5)], axis=1)


def kernel(
    raw_ref, taps_ref, rec_ref, pairs_ref, table_ref, band_ref, out_ref, flag_ref,
    raw, fold, white, marks_out, marks_in, rank, own_rank, pick, send, recv, slot, take, acc, part, parts, whole,
    load_sem, mark_send, mark_recv, row_send, row_recv, part_send, part_recv, whole_send, whole_recv,
):
    t, c = lax.axis_index("tm"), lax.axis_index("chan")
    windows, rows, length = raw.shape
    groups = 16
    team = 8
    pair_count = out_ref.shape[0]
    share = pair_count // team

    for w in range(windows):
        pltpu.make_async_copy(raw_ref.at[w], raw.at[w], load_sem.at[w]).start()

    def chan_peer(k):
        return (c // 4 + k // 4) % 4 * 4 + (c % 4 + k % 4) % 4

    def chan_from(k):
        return (c // 4 + 4 - k // 4) % 4 * 4 + (c % 4 + 4 - k % 4) % 4

    barrier = pltpu.get_barrier_semaphore()

    def greet_chan(k, _):
        pl.semaphore_signal(barrier, inc=1, device_id=(t, chan_peer(k)), device_id_type=MESH)
        return 0

    def greet_tm(k, _):
        pl.semaphore_signal(barrier, inc=1, device_id=((t + k) % team, c), device_id_type=MESH)
        return 0

    lax.fori_loop(1, groups, greet_chan, 0)
    lax.fori_loop(1, team, greet_tm, 0)

    ends = pairs_ref[...]
    high, low = ends // 128, ends % 128
    place = iota((128, pair_count), 0)
    named = jnp.zeros((128, 128), F32)
    for e in range(2):
        named += dot_nt(
            one(low[e : e + 1] == place).astype(BF16), one(high[e : e + 1] == place).astype(BF16)
        )
    named = one(named > 0.0).astype(BF16)
    marks_out[...] = jnp.zeros_like(marks_out)

    def mark(r, _):
        ids = row_of(rec_ref, r * 5)
        place = iota((128, rows), 0)
        found = dot(named, one(ids // 128 == place).astype(BF16))
        line = jnp.sum(jnp.where(ids % 128 == place, found, 0.0), axis=0, keepdims=True)
        for k in range(5):
            marks_out[r, pl.ds(k, 1), :] = line[:, k * 128 : (k + 1) * 128]
        return 0

    lax.fori_loop(0, groups, mark, 0)
    marks = marks_out[...].reshape(128, 128)
    ranks, before = ranks_of(marks)
    own_rank[...] = jnp.where(ranks < CAP, ranks, -1.0)
    sub = iota((128, 128), 0) % 8
    over = jnp.max(jnp.where((sub == 5) & (before > CAP), 1.0, 0.0), axis=0, keepdims=True)
    marks_out[...] = jnp.where(sub == 5, over, marks).reshape(groups, 8, 128)
    marks_in[pl.ds(c, 1)] = marks_out[pl.ds(c, 1)]

    pl.semaphore_wait(barrier, groups + team - 2)

    def mark_copy(k):
        p = chan_peer(k)
        return pltpu.make_async_remote_copy(
            marks_out.at[p], marks_in.at[c], mark_send.at[k], mark_recv.at[k],
            device_id=(t, p), device_id_type=MESH,
        )

    def start_mark(k, _):
        mark_copy(k).start()
        return 0

    lax.fori_loop(1, groups, start_mark, 0)

    shifted = jnp.broadcast_to(
        jnp.concatenate([taps_ref[...].astype(F32), jnp.zeros((1, 128), F32)], axis=1), (128, 256)
    )
    line = iota((128, 256), 0)
    for bit in range(7):
        shifted = jnp.where((line // (1 << bit)) % 2 == 1, pltpu.roll(shifted, 1 << bit, 1), shifted)
    block = shifted.astype(BF16)
    for k in range(length // 128):
        fold[pl.ds(k * 128, 128), :] = dot(block, table_ref[pl.ds(k * 128, 256), :]).astype(BF16)

    bins = iota((1, NB), 1)
    inv_count = 1.0 / (
        jnp.minimum(bins + SMOOTH, NB - 1) - jnp.maximum(bins - SMOOTH, 0) + 1
    ).astype(F32)

    def whiten(w):
        pltpu.make_async_copy(raw_ref.at[w], raw.at[w], load_sem.at[w]).wait()
        for half in range(2):
            here = pl.ds(half * (rows // 2), rows // 2)
            spectrum = dot(raw[w, here, :], fold[...])
            re, im = spectrum[:, :NB], spectrum[:, NB:]
            size = jnp.sqrt(re * re + im * im)
            big = size.astype(BF16)
            rest = (size - big.astype(F32)).astype(BF16)
            sums = dot(jnp.concatenate([big, rest], axis=1), band_ref[...])
            scale = 1.0 / (sums[:, :NB] * inv_count + sums[:, NB:] * (0.1 / NB) + 1e-06)
            white[w, here, :] = jnp.concatenate([re * scale, im * scale], axis=1).astype(BF16)

    def row_copy(w, k):
        p = chan_peer(k)
        return pltpu.make_async_remote_copy(
            send.at[w, p], recv.at[w, c], row_send.at[w, k], row_recv.at[w, k],
            device_id=(t, p), device_id_type=MESH,
        )

    def ship(w):
        send[w] = dot(pick[...], white[w]).astype(BF16).reshape(groups, CAP, 2 * NB)

        def start_row(k, _):
            row_copy(w, k).start()
            return 0

        lax.fori_loop(1, groups, start_row, 0)
        recv[w, pl.ds(c, 1)] = send[w, pl.ds(c, 1)]

    whiten(0)

    def end_mark(k, _):
        mark_copy(k).wait()
        return 0

    lax.fori_loop(1, groups, end_mark, 0)
    asked = marks_in[...].reshape(128, 128)
    flag_ref[...] = jnp.broadcast_to(
        jnp.max(jnp.where(sub == 5, asked, 0.0), axis=0, keepdims=True), (8, 128)
    )
    rank[...] = ranks_of(asked)[0]

    def choose(p, _):
        pick[pl.ds(pl.multiple_of(p * CAP, CAP), CAP), :] = one(
            row_of(rank, p * 8) == iota((CAP, rows), 0).astype(F32)
        ).astype(BF16)
        return 0

    lax.fori_loop(0, groups, choose, 0)
    ship(0)
    for w in range(1, windows):
        whiten(w)
        ship(w)

    def name_slots(j, _):
        found = jnp.zeros((8, 128), F32)
        for h in range(2):
            r = j * 2 + h
            ids = row_of(rec_ref, r * 5)
            ranked = row_of(own_rank, r * 8)
            spot = jnp.where(ranked >= 0.0, ranked + h * CAP, -1.0)
            chosen = one(spot == iota((128, rows), 0).astype(F32)).astype(BF16)
            kind = iota((8, rows), 0)
            values = jnp.where(
                kind == 0, (ids // 128).astype(F32), jnp.where(kind == 1, (ids % 128).astype(F32), 1.0)
            )
            found += dot_nt(values.astype(BF16), chosen)
        slot[pl.ds(j, 1), :] = jnp.where(
            found[2:3] > 0.0, found[0:1] * 128.0 + found[1:2], -1.0
        )
        return 0

    lax.fori_loop(0, groups // 2, name_slots, 0)
    columns = jnp.concatenate([ends.astype(F32), jnp.zeros((6, pair_count), F32)], axis=0).T
    for e in range(2):
        for j in range(groups // 2):
            take[e, :, j * 128 : (j + 1) * 128] = one(
                columns[:, e : e + 1] == slot[j : j + 1, :]
            ).astype(BF16)

    for w in range(windows):

        def end_row(k, _):
            row_copy(w, k).wait()
            return 0

        lax.fori_loop(1, groups, end_row, 0)
        arrived = recv[w].reshape(groups * CAP, 2 * NB)
        a = dot(take[0], arrived)
        b = dot(take[1], arrived)
        are, aim, bre, bim = a[:, :NB], a[:, NB:], b[:, :NB], b[:, NB:]
        product = jnp.concatenate([are * bre + aim * bim, aim * bre - are * bim], axis=1)
        if w == 0:
            acc[...] = product
        elif w < windows - 1:
            acc[...] += product
        else:
            part[...] = (
                ((acc[...] + product) * (1.0 / (windows * team))).astype(BF16).reshape(team, share, 2 * NB)
            )

    def part_copy(k):
        return pltpu.make_async_remote_copy(
            part.at[(t + k) % team], parts.at[t], part_send.at[k], part_recv.at[k],
            device_id=((t + k) % team, c), device_id_type=MESH,
        )

    def whole_copy(k):
        return pltpu.make_async_remote_copy(
            whole.at[t], whole.at[t], whole_send.at[k], whole_recv.at[k],
            device_id=((t + k) % team, c), device_id_type=MESH,
        )

    def start_part(k, _):
        part_copy(k).start()
        return 0

    def end_part(k, _):
        part_copy(k).wait()
        return 0

    def start_whole(k, _):
        whole_copy(k).start()
        return 0

    def end_whole(k, _):
        whole_copy(k).wait()
        return 0

    lax.fori_loop(1, team, start_part, 0)
    parts[pl.ds(t, 1)] = part[pl.ds(t, 1)]
    lax.fori_loop(1, team, end_part, 0)
    whole[pl.ds(t, 1)] = jnp.sum(parts[...].astype(F32), axis=0, keepdims=True).astype(BF16)
    lax.fori_loop(1, team, start_whole, 0)
    lax.fori_loop(1, team, end_whole, 0)
    out_ref[...] = whole[...].reshape(pair_count, 2 * NB).astype(F32)


def general(raw_blocks, fir_taps, recorder_channel, pairs, table, band):
    windows, rows, length = raw_blocks.shape
    offset = jnp.arange(length)[None, :] - jnp.arange(length)[:, None]
    filters = jnp.where(
        (offset >= 0) & (offset < fir_taps.shape[0]),
        jnp.take(fir_taps, jnp.clip(offset, 0, fir_taps.shape[0] - 1)),
        0,
    ).astype(BF16)
    rows_of = jnp.argsort(recorder_channel, stable=True)
    left, right = jnp.take(rows_of, pairs[:, 0]), jnp.take(rows_of, pairs[:, 1])
    smoother = band[:NB, :NB].astype(F32)
    smoother = smoother / jnp.sum(smoother, axis=0, keepdims=True)

    def one_window(total, window):
        filtered = dot(window, filters).astype(BF16)
        spectrum = dot(filtered, table[:length])
        re, im = spectrum[:, :NB], spectrum[:, NB:]
        size = jnp.sqrt(re * re + im * im)
        smoothed = jnp.dot(size, smoother, precision=lax.Precision.HIGHEST)
        scale = 1.0 / (smoothed + 0.1 * jnp.mean(size, axis=-1, keepdims=True) + 1e-06)
        whitened = jnp.concatenate([re * scale, im * scale], axis=1).astype(BF16)
        everything = lax.all_gather(whitened, "chan", axis=0, tiled=True)
        a = jnp.take(everything, left, axis=0).astype(F32)
        b = jnp.take(everything, right, axis=0).astype(F32)
        are, aim, bre, bim = a[:, :NB], a[:, NB:], b[:, :NB], b[:, NB:]
        return total + jnp.concatenate([are * bre + aim * bim, aim * bre - are * bim], axis=1), None

    total, _ = lax.scan(one_window, jnp.zeros((pairs.shape[0], 2 * NB), F32), raw_blocks)
    return lax.psum(total, "tm") / (windows * lax.axis_size("tm"))


def local(raw_blocks, fir_taps, recorder_channel, pairs):
    windows, rows, length = raw_blocks.shape
    pair_count = pairs.shape[0]
    groups, team = 16, 8
    share = pair_count // team
    table = jnp.asarray(table_values(length, 128))
    band = jnp.asarray(band_values())
    vmem = pl.BlockSpec(memory_space=pltpu.VMEM)
    dma = pltpu.SemaphoreType.DMA
    out, flag = pl.pallas_call(
        kernel,
        out_shape=[
            jax.ShapeDtypeStruct((pair_count, 2 * NB), F32),
            jax.ShapeDtypeStruct((8, 128), F32),
        ],
        in_specs=[pl.BlockSpec(memory_space=pl.ANY)] + [vmem] * 5,
        out_specs=[vmem, vmem],
        scratch_shapes=[
            pltpu.VMEM((windows, rows, length), BF16),
            pltpu.VMEM((length, 2 * NB), BF16),
            pltpu.VMEM((windows, rows, 2 * NB), BF16),
            pltpu.VMEM((groups, 8, 128), F32),
            pltpu.VMEM((groups, 8, 128), F32),
            pltpu.VMEM((groups * 8, 128), F32),
            pltpu.VMEM((groups * 8, 128), F32),
            pltpu.VMEM((groups * CAP, rows), BF16),
            pltpu.VMEM((windows, groups, CAP, 2 * NB), BF16),
            pltpu.VMEM((windows, groups, CAP, 2 * NB), BF16),
            pltpu.VMEM((groups // 2, 128), F32),
            pltpu.VMEM((2, pair_count, groups * CAP), BF16),
            pltpu.VMEM((pair_count, 2 * NB), F32),
            pltpu.VMEM((team, share, 2 * NB), BF16),
            pltpu.VMEM((team, share, 2 * NB), BF16),
            pltpu.VMEM((team, share, 2 * NB), BF16),
            dma((windows,)),
            dma((groups,)),
            dma((groups,)),
            dma((windows, groups)),
            dma((windows, groups)),
            dma((team,)),
            dma((team,)),
            dma((team,)),
            dma((team,)),
        ],
        compiler_params=pltpu.CompilerParams(
            collective_id=0, has_side_effects=True, vmem_limit_bytes=48 * 2**20
        ),
    )(raw_blocks, fir_taps.reshape(1, -1), recorder_channel.reshape(-1, 128), pairs.T, table, band)
    return lax.cond(
        flag[0, 0] > 0.0,
        lambda: general(raw_blocks, fir_taps, recorder_channel, pairs, table, band),
        lambda: out,
    )


def solution(mesh):
    in_specs = (P("tm", "chan", None), P(), P(), P("chan", None))
    out_specs = P("chan", None)
    return jax.shard_map(local, mesh=mesh, in_specs=in_specs, out_specs=out_specs, check_vma=False)
```

profile of v0, /device:TPU:1, one launch (start us, length us, event | category | flops | bytes accessed | tf_op | source)
XLA Modules:
  0.0 71.5 jit_solution(10828524207663053541)
XLA Ops:
  6.5 0.0 copy-start.3
  6.5 0.0 copy-start
  6.5 0.0 copy-start.4
  6.5 0.0 copy-start.10
  6.5 54.8 %shard_map.66 = (f32[512,256]{1,0:T(8,128)}, f32[8,128]{1,0:T(8,128)S(1)}) custom-call(bf16[4,640,1024]{2,1,0:T(8,128)(2,1)} %raw_ref.1, bf16[1,128]{1,0:T(2,128)(2,1)} %bitcast.23, s32[80,128]{1,0:T(8,128)} %bitcast.25, s32[2,512]{1,0:T(2,128)} %bitcast.30, bf16[1152,256]{1,0:T(8,128)(2,1)} %constant.95.clone.table_ref, ...), custom_call_target="tpu_custom_call" | custom-call | tf_op jit(solution)/shard_map/pallas_call | solution.py:335
  61.4 0.5 slice.54
  62.5 0.0 copy-done.3
  62.6 0.0 copy-done
  62.6 0.0 copy-done.4
  62.6 0.0 copy-done.10
  62.6 0.2 conditional.1
  62.8 1.9 %copy.26 = f32[512,256]{1,0:T(8,128)} copy(f32[512,256]{1,0:T(8,128)} %get-tuple-element.135) | data formatting | bytes 1048576
Async XLA Ops:
  6.5 56.0 %copy-start.3 = (bf16[256,256]{1,0:T(8,128)(2,1)S(1)}, bf16[256,256]{1,0:T(8,128)(2,1)}, u32[]{:S(2)}) copy-start(bf16[256,256]{1,0:T(8,128)(2,1)} %constant.96.clone.band_ref) | copy-start | bytes 393220
  6.5 56.0 %copy-start = (bf16[128]{0:T(256)(128)(2,1)S(1)}, bf16[128]{0:T(256)(128)(2,1)}, u32[]{:S(2)}) copy-start(bf16[128]{0:T(256)(128)(2,1)} %param.15) | copy-start | bytes 772
  6.5 56.0 %copy-start.4 = (s32[10240]{0:T(1024)S(1)}, s32[10240]{0:T(1024)}, u32[]{:S(2)}) copy-start(s32[10240]{0:T(1024)} %param.16) | copy-start | bytes 122884
  6.5 56.0 %copy-start.10 = (s32[512,2]{0,1:T(2,128)S(1)}, s32[512,2]{0,1:T(2,128)}, u32[]{:S(2)}) copy-start(s32[512,2]{0,1:T(2,128)} %param.17) | copy-start | bytes 12292
where the time goes:
time: 71.7 us; the launch traced here: 71.5 us
  Pallas kernels  54.8 us (76%)
  between operations  14.1 us (20%)
  local copies, waits for them, and re-layouts  2.4 us (3%)
    pallas_call x1, Pallas kernels, local(): pl.pallas_call(kernel, out_shape=[jax.ShapeDtypeStruct((pair_count, 2 * N...  54.8 us
    unnamed x9, local copies, waits for them, and re-layouts  1.88 us

commit v1 on v0

v1 whole, which is shorter than its diff:
```python
import jax
import jax.numpy as jnp
import numpy as np
from jax import lax
from jax.experimental import pallas as pl
from jax.experimental.pallas import tpu as pltpu
from jax.sharding import PartitionSpec as P

NB = 128
SMOOTH = 4
CAP = 56
SLOT = 64
MESH = pl.DeviceIdType.MESH
F32 = jnp.float32
BF16 = jnp.bfloat16
NT = (((1,), (1,)), ((), ()))


def table_values(length, extra):
    samples = np.arange(length, dtype=np.int64)
    freqs = np.arange(1, NB + 1, dtype=np.int64)
    angles = (samples[:, None] * freqs[None, :] % length).astype(np.float32) * np.float32(2.0 * np.pi / length)
    table = np.concatenate([np.cos(angles), -np.sin(angles)], axis=1)
    return np.concatenate([table, np.zeros((extra, 2 * NB), np.float32)]).astype(BF16)


def iota(shape, dim):
    return lax.broadcasted_iota(jnp.int32, shape, dim)


def dot(left, right):
    return jnp.dot(left, right, preferred_element_type=F32)


def dot_nt(left, right):
    return lax.dot_general(left, right, NT, preferred_element_type=F32)


def one(condition):
    return jnp.where(condition, 1.0, 0.0)


def ranks_of(marks):
    row, col = iota((128, 128), 0), iota((128, 128), 1)
    marks = jnp.where(row % 8 < 5, marks, 0.0)
    held = marks.astype(BF16)
    upto = dot(held, one(row <= col).astype(BF16))
    totals = dot(held, jnp.ones((128, 128), BF16))
    before = dot(one((row // 8 == col // 8) & (col < row)).astype(BF16), totals.astype(BF16))
    return jnp.where(marks > 0.0, upto + before - 1.0, -1.0), before


def row_of(ref, first):
    return jnp.concatenate([ref[pl.ds(first + k, 1), :] for k in range(5)], axis=1)


def roll_half(value):
    return pltpu.roll(value, NB // 2, 1)


def kernel(
    raw_hbm, taps_hbm, rec_hbm, pairs_hbm, table_hbm, out_ref, flag_ref,
    raw, taps, rec, pairs, table, fold, white, marks_out, marks_in, rank, own_rank, send, recv, arrived, slot, take,
    part, parts, whole,
    load_sem, small_sem, mark_send, mark_recv, row_send, row_recv, part_send, part_recv, whole_send, whole_recv,
):
    t, c = lax.axis_index("tm"), lax.axis_index("chan")
    y, z = c // 4, c % 4
    windows, rows, length = raw.shape
    groups = 16
    team = 8
    pair_count = out_ref.shape[0]
    share = pair_count // team

    small = [(pairs_hbm, pairs), (rec_hbm, rec), (taps_hbm, taps), (table_hbm, table)]

    def small_copy(i):
        return pltpu.make_async_copy(small[i][0], small[i][1], small_sem.at[i])

    def load_copy(w):
        return pltpu.make_async_copy(raw_hbm.at[w], raw.at[w], load_sem.at[w])

    for i in range(len(small)):
        small_copy(i).start()
    for w in range(windows):
        load_copy(w).start()

    def chan_peer(k):
        return (y + k // 4) % 4 * 4 + (z + k % 4) % 4

    def chan_from(k):
        return (y + 4 - k // 4) % 4 * 4 + (z + 4 - k % 4) % 4

    barrier = pltpu.get_barrier_semaphore()

    def greet_chan(k, _):
        pl.semaphore_signal(barrier, inc=1, device_id=(t, chan_peer(k)), device_id_type=MESH)
        return 0

    def greet_tm(k, _):
        pl.semaphore_signal(barrier, inc=1, device_id=((t + k) % team, c), device_id_type=MESH)
        return 0

    lax.fori_loop(1, groups, greet_chan, 0)
    lax.fori_loop(1, team, greet_tm, 0)

    small_copy(0).wait()
    ends = pairs[...]
    high, low = ends // 128, ends % 128
    place = iota((128, pair_count), 0)
    named = jnp.zeros((128, 128), F32)
    for e in range(2):
        named += dot_nt(
            one(low[e : e + 1] == place).astype(BF16), one(high[e : e + 1] == place).astype(BF16)
        )
    named = one(named > 0.0).astype(BF16)
    marks_out[...] = jnp.zeros_like(marks_out)
    small_copy(1).wait()

    def mark(j, _):
        ids = jnp.concatenate([rec[pl.ds(j * 10 + k, 1), :] for k in range(10)], axis=1)
        place = iota((128, 2 * rows), 0)
        found = dot(named, one(ids // 128 == place).astype(BF16))
        line = jnp.sum(jnp.where(ids % 128 == place, found, 0.0), axis=0, keepdims=True)
        for k in range(10):
            marks_out[j * 2 + k // 5, pl.ds(k % 5, 1), :] = line[:, k * 128 : (k + 1) * 128]
        return 0

    lax.fori_loop(0, groups // 2, mark, 0)
    marks = marks_out[...].reshape(128, 128)
    ranks, before = ranks_of(marks)
    own_rank[...] = jnp.where(ranks < CAP, ranks, -1.0)
    sub = iota((128, 128), 0) % 8
    over = jnp.max(jnp.where((sub == 5) & (before > CAP), 1.0, 0.0), axis=0, keepdims=True)
    marks_out[...] = jnp.where(sub == 5, over, marks).reshape(groups, 8, 128)
    marks_in[pl.ds(c, 1)] = marks_out[pl.ds(c, 1)]

    pl.semaphore_wait(barrier, groups + team - 2)

    def mark_copy(k):
        p = chan_peer(k)
        return pltpu.make_async_remote_copy(
            marks_out.at[p], marks_in.at[c], mark_send.at[k], mark_recv.at[k],
            device_id=(t, p), device_id_type=MESH,
        )

    def start_mark(k, _):
        mark_copy(k).start()
        return 0

    lax.fori_loop(1, groups, start_mark, 0)

    small_copy(2).wait()
    shifted = jnp.broadcast_to(
        jnp.concatenate([taps[...].astype(F32), jnp.zeros((1, 128), F32)], axis=1), (128, 256)
    )
    line = iota((128, 256), 0)
    for bit in range(7):
        shifted = jnp.where((line // (1 << bit)) % 2 == 1, pltpu.roll(shifted, 1 << bit, 1), shifted)
    block = shifted.astype(BF16)
    small_copy(3).wait()
    for k in range(length // 128):
        fold[pl.ds(k * 128, 128), :] = dot(block, table[pl.ds(k * 128, 256), :]).astype(BF16)

    bins = iota((1, NB), 1)
    inv_count = 1.0 / (
        jnp.minimum(bins + SMOOTH, NB - 1) - jnp.maximum(bins - SMOOTH, 0) + 1
    ).astype(F32)
    from_bin, to_bin = iota((2 * NB, 2 * NB), 0) % NB, iota((2 * NB, 2 * NB), 1)
    near = (from_bin - to_bin <= SMOOTH) & (to_bin - from_bin <= SMOOTH)
    band = one(near | (to_bin >= NB)).astype(BF16)
    lower = iota((rows // 2, NB), 1) < NB // 2

    for w in range(windows):
        load_copy(w).wait()
        for half in range(2):
            here = pl.ds(half * (rows // 2), rows // 2)
            spectrum = dot(raw[w, here, :], fold[...])
            re, im = spectrum[:, :NB], spectrum[:, NB:]
            size = jnp.sqrt(re * re + im * im)
            big = size.astype(BF16)
            rest = (size - big.astype(F32)).astype(BF16)
            sums = dot(jnp.concatenate([big, rest], axis=1), band)
            scale = 1.0 / (sums[:, :NB] * inv_count + sums[:, NB:] * (0.1 / NB) + 1e-06)
            re, im = re * scale, im * scale
            lanes = pl.ds(w * NB, NB)
            white[0, here, lanes] = jnp.where(lower, re, roll_half(im)).astype(BF16)
            white[1, here, lanes] = jnp.where(lower, roll_half(re), im).astype(BF16)

    def end_mark(k, _):
        mark_copy(k).wait_recv()
        return 0

    lax.fori_loop(1, groups, end_mark, 0)
    asked = marks_in[...].reshape(128, 128)
    flag_ref[...] = jnp.broadcast_to(
        jnp.max(jnp.where(sub == 5, asked, 0.0), axis=0, keepdims=True), (8, 128)
    )
    rank[...] = ranks_of(asked)[0]

    def row_copy(h, k):
        p = chan_peer(k)
        return pltpu.make_async_remote_copy(
            send.at[h, p], recv.at[h, c], row_send.at[h, k], row_recv.at[h, k],
            device_id=(t, p), device_id_type=MESH,
        )

    def ship(h):
        for k in (8, 4, 12, 0):
            picks = []
            for m in range(4):
                ranked = row_of(rank, chan_peer(k + m) * 8)
                picks.append(one(ranked == iota((CAP, rows), 0).astype(F32)))
            chosen = dot(jnp.concatenate(picks, axis=0).astype(BF16), white[h])
            for m in range(4):
                mine = chosen[m * CAP : (m + 1) * CAP]
                send[h, pl.ds(chan_peer(k + m), 1)] = jnp.concatenate(
                    [mine[:, : 2 * NB], mine[:, 2 * NB :]], axis=0
                ).astype(BF16)[None]
            for m in (2, 1, 3, 0):
                if k + m:
                    row_copy(h, k + m).start()

    ship(0)
    ship(1)

    def name_slots(j, _):
        found = jnp.zeros((8, 128), F32)
        for h in range(2):
            r = j * 2 + h
            ids = row_of(rec, r * 5)
            ranked = row_of(own_rank, r * 8)
            spot = jnp.where(ranked >= 0.0, ranked + h * SLOT, -1.0)
            chosen = one(spot == iota((128, rows), 0).astype(F32)).astype(BF16)
            kind = iota((8, rows), 0)
            values = jnp.where(
                kind == 0, (ids // 128).astype(F32), jnp.where(kind == 1, (ids % 128).astype(F32), 1.0)
            )
            found += dot_nt(values.astype(BF16), chosen)
        slot[pl.ds(j, 1), :] = jnp.where(
            found[2:3] > 0.0, found[0:1] * 128.0 + found[1:2], -1.0
        )
        return 0

    lax.fori_loop(0, groups // 2, name_slots, 0)
    columns = jnp.concatenate([ends.astype(F32), jnp.zeros((6, pair_count), F32)], axis=0).T
    for e in range(2):
        for j in range(groups // 2):
            take[e, :, j * 128 : (j + 1) * 128] = one(
                columns[:, e : e + 1] == slot[j : j + 1, :]
            ).astype(BF16)

    def part_copy(h, k):
        return pltpu.make_async_remote_copy(
            part.at[h, (t + k) % team], parts.at[h, t], part_send.at[h, k], part_recv.at[h, k],
            device_id=((t + k) % team, c), device_id_type=MESH,
        )

    def whole_copy(h, k):
        return pltpu.make_async_remote_copy(
            whole.at[h, t], whole.at[h, t], whole_send.at[h, k], whole_recv.at[h, k],
            device_id=((t + k) % team, c), device_id_type=MESH,
        )

    def settle(h, r):
        got = recv[h, pl.ds(r, 1)][0].astype(F32)
        arrived[pl.ds(pl.multiple_of(r * SLOT, SLOT), SLOT), :] = jnp.concatenate(
            [
                jnp.concatenate([got[:CAP], got[CAP:]], axis=1),
                jnp.zeros((SLOT - CAP, 4 * NB), F32),
            ],
            axis=0,
        ).astype(BF16)

    for h in range(2):
        recv[h, pl.ds(c, 1)] = send[h, pl.ds(c, 1)]
        settle(h, c)

        def end_row(k, _, h=h):
            row_copy(h, k).wait_recv()
            settle(h, chan_from(k))
            return 0

        lax.fori_loop(1, groups, end_row, 0)
        for q in range(2):
            some = pl.ds(q * (pair_count // 2), pair_count // 2)
            a = dot(take[0, some, :], arrived[...])
            b = dot(take[1, some, :], arrived[...])
            straight = jnp.zeros((pair_count // 2, NB), F32)
            crossed = jnp.zeros((pair_count // 2, NB), F32)
            for w in range(windows):
                aw, bw = a[:, w * NB : (w + 1) * NB], b[:, w * NB : (w + 1) * NB]
                straight += aw * bw
                crossed += aw * roll_half(bw)
            lower = iota((pair_count // 2, NB), 1) < NB // 2
            product = jnp.where(lower, straight + roll_half(straight), crossed - roll_half(crossed))
            part[h, pl.ds(q * (team // 2), team // 2)] = (
                (product * (1.0 / (windows * team))).astype(BF16).reshape(team // 2, share, NB)
            )

        def start_part(k, _, h=h):
            part_copy(h, k).start()
            return 0

        def end_part(k, _, h=h):
            part_copy(h, k).wait_recv()
            return 0

        def start_whole(k, _, h=h):
            whole_copy(h, k).start()
            return 0

        lax.fori_loop(1, team, start_part, 0)
        parts[h, pl.ds(t, 1)] = part[h, pl.ds(t, 1)]
        lax.fori_loop(1, team, end_part, 0)
        whole[h, pl.ds(t, 1)] = jnp.sum(parts[h].astype(F32), axis=0, keepdims=True).astype(BF16)
        lax.fori_loop(1, team, start_whole, 0)

    def end_whole(k, _):
        for h in range(2):
            whole_copy(h, k).wait_recv()
        return 0

    lax.fori_loop(1, team, end_whole, 0)
    first = whole[0].astype(F32).reshape(pair_count, NB)
    second = whole[1].astype(F32).reshape(pair_count, NB)
    lower = iota((pair_count, NB), 1) < NB // 2
    out_ref[:, :NB] = jnp.where(lower, first, roll_half(second))
    out_ref[:, NB:] = jnp.where(lower, roll_half(first), second)

    def end_sends(k, _):
        mark_copy(k).wait_send()
        for h in range(2):
            row_copy(h, k).wait_send()
        return 0

    def end_team_sends(k, _):
        for h in range(2):
            part_copy(h, k).wait_send()
            whole_copy(h, k).wait_send()
        return 0

    lax.fori_loop(1, groups, end_sends, 0)
    lax.fori_loop(1, team, end_team_sends, 0)


def spread(block, axis):
    count = lax.axis_size(axis)
    return lax.all_to_all(jnp.broadcast_to(block[None], (count,) + block.shape), axis, 0, 0)


def general(raw_blocks, fir_taps, recorder_channel, pairs, table):
    windows, rows, length = raw_blocks.shape
    offset = jnp.arange(length)[None, :] - jnp.arange(length)[:, None]
    filters = jnp.where(
        (offset >= 0) & (offset < fir_taps.shape[0]),
        jnp.take(fir_taps, jnp.clip(offset, 0, fir_taps.shape[0] - 1)),
        0,
    ).astype(BF16)
    channels = recorder_channel.shape[0]
    rows_of = jnp.zeros((channels,), jnp.int32).at[recorder_channel].set(jnp.arange(channels, dtype=jnp.int32))
    left, right = jnp.take(rows_of, pairs[:, 0]), jnp.take(rows_of, pairs[:, 1])
    bins = jnp.arange(NB)
    near = (jnp.abs(bins[:, None] - bins[None, :]) <= SMOOTH).astype(F32)
    smoother = near / jnp.sum(near, axis=0, keepdims=True)

    def one_window(total, window):
        filtered = dot(window, filters).astype(BF16)
        spectrum = dot(filtered, table[:length])
        re, im = spectrum[:, :NB], spectrum[:, NB:]
        size = jnp.sqrt(re * re + im * im)
        smoothed = jnp.dot(size, smoother, precision=lax.Precision.HIGHEST)
        scale = 1.0 / (smoothed + 0.1 * jnp.mean(size, axis=-1, keepdims=True) + 1e-06)
        whitened = jnp.concatenate([re * scale, im * scale], axis=1).astype(BF16)
        everything = spread(whitened, "chan").reshape(channels, 2 * NB)
        a = jnp.take(everything, left, axis=0).astype(F32)
        b = jnp.take(everything, right, axis=0).astype(F32)
        are, aim, bre, bim = a[:, :NB], a[:, NB:], b[:, :NB], b[:, NB:]
        return total + jnp.concatenate([are * bre + aim * bim, aim * bre - are * bim], axis=1), None

    total, _ = lax.scan(one_window, jnp.zeros((pairs.shape[0], 2 * NB), F32), raw_blocks)
    return jnp.sum(spread(total, "tm"), axis=0) / (windows * lax.axis_size("tm"))


def local(raw_blocks, fir_taps, recorder_channel, pairs):
    windows, rows, length = raw_blocks.shape
    pair_count = pairs.shape[0]
    groups, team = 16, 8
    share = pair_count // team
    table = jnp.asarray(table_values(length, 128))
    hbm = pl.BlockSpec(memory_space=pltpu.HBM)
    vmem = pl.BlockSpec(memory_space=pltpu.VMEM)
    dma = pltpu.SemaphoreType.DMA
    out, flag = pl.pallas_call(
        kernel,
        out_shape=[
            jax.ShapeDtypeStruct((pair_count, 2 * NB), F32),
            jax.ShapeDtypeStruct((8, 128), F32),
        ],
        in_specs=[hbm] * 5,
        out_specs=[vmem, vmem],
        scratch_shapes=[
            pltpu.VMEM((windows, rows, length), BF16),
            pltpu.VMEM((1, 128), BF16),
            pltpu.VMEM((80, 128), jnp.int32),
            pltpu.VMEM((2, pair_count), jnp.int32),
            pltpu.VMEM((length + 128, 2 * NB), BF16),
            pltpu.VMEM((length, 2 * NB), BF16),
            pltpu.VMEM((2, rows, windows * NB), BF16),
            pltpu.VMEM((groups, 8, 128), F32),
            pltpu.VMEM((groups, 8, 128), F32),
            pltpu.VMEM((groups * 8, 128), F32),
            pltpu.VMEM((groups * 8, 128), F32),
            pltpu.VMEM((2, groups, 2 * CAP, 2 * NB), BF16),
            pltpu.VMEM((2, groups, 2 * CAP, 2 * NB), BF16),
            pltpu.VMEM((groups * SLOT, windows * NB), BF16),
            pltpu.VMEM((groups // 2, 128), F32),
            pltpu.VMEM((2, pair_count, groups * SLOT), BF16),
            pltpu.VMEM((2, team, share, NB), BF16),
            pltpu.VMEM((2, team, share, NB), BF16),
            pltpu.VMEM((2, team, share, NB), BF16),
            dma((windows,)),
            dma((4,)),
            dma((groups,)),
            dma((groups,)),
            dma((2, groups)),
            dma((2, groups)),
            dma((2, team)),
            dma((2, team)),
            dma((2, team)),
            dma((2, team)),
        ],
        compiler_params=pltpu.CompilerParams(
            collective_id=0, has_side_effects=True, vmem_limit_bytes=40 * 2**20
        ),
    )(raw_blocks, fir_taps.reshape(1, -1), recorder_channel.reshape(-1, 128), pairs.T, table)
    return lax.cond(
        flag[0, 0] > 0.0,
        lambda: general(raw_blocks, fir_taps, recorder_channel, pairs, table),
        lambda: out,
    )


def solution(mesh):
    in_specs = (P("tm", "chan", None), P(), P(), P("chan", None))
    out_specs = P("chan", None)
    return jax.shard_map(local, mesh=mesh, in_specs=in_specs, out_specs=out_specs, check_vma=False)
```

time: 71.7 us -> 53.6 us (0.75)
  between operations: 14.1 us -> 0.7 us
  Pallas kernels: 54.8 us -> 50.1 us
    pallas_call x1, Pallas kernels: 54.8 us -> 50.1 us  [local(): pl.pallas_call(kernel, out_shape=[jax.ShapeDtypeStruct((pair_count, 2 * N...]
    unnamed x9 -> x7, local copies, waits for them, and re-layouts: 1.88 us -> 1.88 us
where the time goes in v1:
time: 53.6 us; the launch traced here: 53.5 us
  Pallas kernels  50.1 us (93%)
  local copies, waits for them, and re-layouts  2.39 us (4%)
  between operations  0.7 us (1%)
    pallas_call x1, Pallas kernels, local(): pl.pallas_call(kernel, out_shape=[jax.ShapeDtypeStruct((pair_count, 2 * N...  50.1 us
    unnamed x7, local copies, waits for them, and re-layouts  1.88 us

profile of v1, /device:TPU:1, one launch (start us, length us, event | category | flops | bytes accessed | tf_op | source)
XLA Modules:
  0.0 53.5 jit_solution(13842739391527265321)
XLA Ops:
  0.0 0.0 copy-start
  0.0 0.0 copy-start.2
  0.0 0.0 copy-start.7
  0.0 50.1 %shard_map.57 = (f32[512,256]{1,0:T(8,128)}, f32[8,128]{1,0:T(8,128)S(1)}) custom-call(bf16[4,640,1024]{2,1,0:T(8,128)(2,1)} %raw_hbm.1, bf16[1,128]{1,0:T(2,128)(2,1)} %bitcast.23, s32[80,128]{1,0:T(8,128)} %bitcast.25, s32[2,512]{1,0:T(2,128)} %bitcast.30, bf16[1152,256]{1,0:T(8,128)(2,1)} %constant.98.clone.table_hbm), custom_call_target="tpu_custom_call" | custom-call | tf_op jit(solution)/shard_map/pallas_call | solution.py:394
  50.2 0.5 slice.51
  51.3 0.0 copy-done
  51.3 0.0 copy-done.2
  51.4 0.0 copy-done.7
  51.4 0.2 conditional.1
  51.6 1.9 %copy.23 = f32[512,256]{1,0:T(8,128)} copy(f32[512,256]{1,0:T(8,128)} %get-tuple-element.131) | data formatting | bytes 1048576
Async XLA Ops:
  0.0 51.3 %copy-start = (bf16[128]{0:T(256)(128)(2,1)S(1)}, bf16[128]{0:T(256)(128)(2,1)}, u32[]{:S(2)}) copy-start(bf16[128]{0:T(256)(128)(2,1)} %param.14) | copy-start | bytes 772
  0.0 51.3 %copy-start.2 = (s32[10240]{0:T(1024)S(1)}, s32[10240]{0:T(1024)}, u32[]{:S(2)}) copy-start(s32[10240]{0:T(1024)} %param.15) | copy-start | bytes 122884
  0.0 51.3 %copy-start.7 = (s32[512,2]{0,1:T(2,128)S(1)}, s32[512,2]{0,1:T(2,128)}, u32[]{:S(2)}) copy-start(s32[512,2]{0,1:T(2,128)} %param.16) | copy-start | bytes 12292

commit v2 on v1

--- a/solution.py
+++ b/solution.py
@@ -193,9 +193,7 @@
 
     lax.fori_loop(1, groups, end_mark, 0)
     asked = marks_in[...].reshape(128, 128)
-    flag_ref[...] = jnp.broadcast_to(
-        jnp.max(jnp.where(sub == 5, asked, 0.0), axis=0, keepdims=True), (8, 128)
-    )
+    flag_ref[0] = jnp.max(jnp.where(sub == 5, asked, 0.0))
     rank[...] = ranks_of(asked)[0]
 
     def row_copy(h, k):
@@ -250,10 +248,10 @@
                 columns[:, e : e + 1] == slot[j : j + 1, :]
             ).astype(BF16)
 
-    def part_copy(h, k):
+    def part_copy(h, to, source):
         return pltpu.make_async_remote_copy(
-            part.at[h, (t + k) % team], parts.at[h, t], part_send.at[h, k], part_recv.at[h, k],
-            device_id=((t + k) % team, c), device_id_type=MESH,
+            part.at[h, to], parts.at[h, source], part_send.at[h, to], part_recv.at[h, source],
+            device_id=(to, c), device_id_type=MESH,
         )
 
     def whole_copy(h, k):
@@ -272,6 +270,20 @@
             axis=0,
         ).astype(BF16)
 
+    def add_parts(h):
+        def end_part(k, _):
+            part_copy(h, 0, (t + k) % team).wait_recv()
+            return 0
+
+        def start_whole(k, _):
+            whole_copy(h, k).start()
+            return 0
+
+        parts[h, pl.ds(t, 1)] = part[h, pl.ds(t, 1)]
+        lax.fori_loop(1, team, end_part, 0)
+        whole[h, pl.ds(t, 1)] = jnp.sum(parts[h].astype(F32), axis=0, keepdims=True).astype(BF16)
+        lax.fori_loop(1, team, start_whole, 0)
+
     for h in range(2):
         recv[h, pl.ds(c, 1)] = send[h, pl.ds(c, 1)]
         settle(h, c)
@@ -282,6 +294,8 @@
             return 0
 
         lax.fori_loop(1, groups, end_row, 0)
+        if h:
+            add_parts(0)
         for q in range(2):
             some = pl.ds(q * (pair_count // 2), pair_count // 2)
             a = dot(take[0, some, :], arrived[...])
@@ -298,23 +312,15 @@
                 (product * (1.0 / (windows * team))).astype(BF16).reshape(team // 2, share, NB)
             )
 
-        def start_part(k, _, h=h):
-            part_copy(h, k).start()
-            return 0
-
-        def end_part(k, _, h=h):
-            part_copy(h, k).wait_recv()
-            return 0
-
-        def start_whole(k, _, h=h):
-            whole_copy(h, k).start()
-            return 0
-
-        lax.fori_loop(1, team, start_part, 0)
-        parts[h, pl.ds(t, 1)] = part[h, pl.ds(t, 1)]
-        lax.fori_loop(1, team, end_part, 0)
-        whole[h, pl.ds(t, 1)] = jnp.sum(parts[h].astype(F32), axis=0, keepdims=True).astype(BF16)
-        lax.fori_loop(1, team, start_whole, 0)
+            def start_part(k, _, h=h):
+                @pl.when(k != t)
+                def _():
+                    part_copy(h, k, t).start()
+
+                return 0
+
+            lax.fori_loop(q * (team // 2), (q + 1) * (team // 2), start_part, 0)
+    add_parts(1)
 
     def end_whole(k, _):
         for h in range(2):
@@ -325,8 +331,8 @@
     first = whole[0].astype(F32).reshape(pair_count, NB)
     second = whole[1].astype(F32).reshape(pair_count, NB)
     lower = iota((pair_count, NB), 1) < NB // 2
-    out_ref[:, :NB] = jnp.where(lower, first, roll_half(second))
-    out_ref[:, NB:] = jnp.where(lower, roll_half(first), second)
+    out_ref[:, :NB] = jnp.where(lower, first, roll_half(second)).astype(BF16)
+    out_ref[:, NB:] = jnp.where(lower, roll_half(first), second).astype(BF16)
 
     def end_sends(k, _):
         mark_copy(k).wait_send()
@@ -336,7 +342,7 @@
 
     def end_team_sends(k, _):
         for h in range(2):
-            part_copy(h, k).wait_send()
+            part_copy(h, (t + k) % team, t).wait_send()
             whole_copy(h, k).wait_send()
         return 0
 
@@ -394,11 +400,11 @@
     out, flag = pl.pallas_call(
         kernel,
         out_shape=[
-            jax.ShapeDtypeStruct((pair_count, 2 * NB), F32),
-            jax.ShapeDtypeStruct((8, 128), F32),
+            jax.ShapeDtypeStruct((pair_count, 2 * NB), BF16),
+            jax.ShapeDtypeStruct((1,), F32),
         ],
         in_specs=[hbm] * 5,
-        out_specs=[vmem, vmem],
+        out_specs=[vmem, pl.BlockSpec(memory_space=pltpu.SMEM)],
         scratch_shapes=[
             pltpu.VMEM((windows, rows, length), BF16),
             pltpu.VMEM((1, 128), BF16),
@@ -435,9 +441,9 @@
         ),
     )(raw_blocks, fir_taps.reshape(1, -1), recorder_channel.reshape(-1, 128), pairs.T, table)
     return lax.cond(
-        flag[0, 0] > 0.0,
+        flag[0] > 0.0,
         lambda: general(raw_blocks, fir_taps, recorder_channel, pairs, table),
-        lambda: out,
+        lambda: out.astype(F32),
     )
 
 

time: 53.6 us -> 51.8 us (0.966)
  local copies, waits for them, and re-layouts: 2.39 us -> 0.01 us
  other arithmetic: 0 us -> 0.83 us
    unnamed x7 -> x6, local copies, waits for them, and re-layouts: 1.88 us -> 0.01 us
    convert_element_type x0 -> x1, other arithmetic: none -> 0.83 us  [local(): out.astype(F32)]
where the time goes in v2:
time: 51.8 us; the launch traced here: 51.7 us
  Pallas kernels  50.2 us (97%)
  other arithmetic  0.83 us (2%)
  between operations  0.67 us (1%)
    pallas_call x1, Pallas kernels, local(): pl.pallas_call(kernel, out_shape=[jax.ShapeDtypeStruct((pair_count, 2 * N...  50.2 us

profile of v2, /device:TPU:1, one launch (start us, length us, event | category | flops | bytes accessed | tf_op | source)
XLA Modules:
  0.0 51.7 jit_solution(9544247825689013409)
XLA Ops:
  0.0 0.0 copy-start
  0.0 0.0 copy-start.2
  0.0 0.0 copy-start.7
  0.0 50.2 %shard_map.57 = (bf16[512,256]{1,0:T(8,128)(2,1)S(1)}, f32[1]{0:T(128)}) custom-call(bf16[4,640,1024]{2,1,0:T(8,128)(2,1)} %raw_hbm.1, bf16[1,128]{1,0:T(2,128)(2,1)} %bitcast.23, s32[80,128]{1,0:T(8,128)} %bitcast.25, s32[2,512]{1,0:T(2,128)} %bitcast.30, bf16[1152,256]{1,0:T(8,128)(2,1)} %constant.98.clone.table_hbm), custom_call_target="tpu_custom_call" | custom-call | tf_op jit(solution)/shard_map/pallas_call | solution.py:400
  50.9 0.0 copy-done
  50.9 0.0 copy-done.2
  50.9 0.0 copy-done.7
  50.9 0.8 %conditional.1 = (f32[512,256]{1,0:T(8,128)}) conditional(s32[]{:T(128)} %bitcast.5, bf16[512,256]{1,0:T(8,128)(2,1)S(1)} %get-tuple-element.130, (bf16[128]{0:T(256)(128)(2,1)S(1)}, s32[10240]{0:T(1024)S(1)}, s32[512,2]{0,1:T(2,128)S(1)}, bf16[4,640,1024]{2,1,0:T(8,128)(2,1)}, bf16[1152,256]{1,0:T(8,128)(2,1)}) %tuple.62), branch_computations={%region_0.0_spmd, %region_1.10_spmd} | conditional | flops 1828508544 | bytes 94291416 | solution.py:443
  50.9 0.8 %convert_element_type.34 = f32[512,256]{1,0:T(8,128)} convert(bf16[512,256]{1,0:T(8,128)(2,1)S(1)} %param) | non-fusion elementwise | flops 131072 | bytes 786432 | tf_op jit(solution)/shard_map/cond/branch_0_fun/convert_element_type | solution.py:446
Async XLA Ops:
  0.0 50.9 %copy-start = (bf16[128]{0:T(256)(128)(2,1)S(1)}, bf16[128]{0:T(256)(128)(2,1)}, u32[]{:S(2)}) copy-start(bf16[128]{0:T(256)(128)(2,1)} %param.14) | copy-start | bytes 772
  0.0 50.9 %copy-start.2 = (s32[10240]{0:T(1024)S(1)}, s32[10240]{0:T(1024)}, u32[]{:S(2)}) copy-start(s32[10240]{0:T(1024)} %param.15) | copy-start | bytes 122884
  0.0 50.9 %copy-start.7 = (s32[512,2]{0,1:T(2,128)S(1)}, s32[512,2]{0,1:T(2,128)}, u32[]{:S(2)}) copy-start(s32[512,2]{0,1:T(2,128)} %param.16) | copy-start | bytes 12292

commit v3 on v2

--- a/solution.py
+++ b/solution.py
@@ -8,8 +8,9 @@
 
 NB = 128
 SMOOTH = 4
-CAP = 56
-SLOT = 64
+CAP1 = 160
+CAP2 = 176
+SLOT = 256
 MESH = pl.DeviceIdType.MESH
 F32 = jnp.float32
 BF16 = jnp.bfloat16
@@ -40,14 +41,14 @@
     return jnp.where(condition, 1.0, 0.0)
 
 
-def ranks_of(marks):
-    row, col = iota((128, 128), 0), iota((128, 128), 1)
-    marks = jnp.where(row % 8 < 5, marks, 0.0)
+def ranks_of(marks, group):
+    count = marks.shape[0]
     held = marks.astype(BF16)
-    upto = dot(held, one(row <= col).astype(BF16))
+    upto = dot(held, one(iota((128, 128), 0) <= iota((128, 128), 1)).astype(BF16))
     totals = dot(held, jnp.ones((128, 128), BF16))
-    before = dot(one((row // 8 == col // 8) & (col < row)).astype(BF16), totals.astype(BF16))
-    return jnp.where(marks > 0.0, upto + before - 1.0, -1.0), before
+    row, col = iota((count, count), 0), iota((count, count), 1)
+    before = dot(one((row // group == col // group) & (col < row)).astype(BF16), totals.astype(BF16))
+    return jnp.where(marks > 0.0, upto + before - 1.0, -1.0)
 
 
 def row_of(ref, first):
@@ -60,14 +61,16 @@
 
 def kernel(
     raw_hbm, taps_hbm, rec_hbm, pairs_hbm, table_hbm, out_ref, flag_ref,
-    raw, taps, rec, pairs, table, fold, white, marks_out, marks_in, rank, own_rank, send, recv, arrived, slot, take,
-    part, parts, whole,
-    load_sem, small_sem, mark_send, mark_recv, row_send, row_recv, part_send, part_recv, whole_send, whole_recv,
+    raw, taps, rec, pairs, table, fold, white, marks, inner, union, wanted, own_rank, inner_rank, union_rank, wanted_rank,
+    pick1, pick2, send1, recv1, send2, recv2, slot, take, part, parts, whole, flags,
+    load_sem, small_sem, ask1_send, ask1_recv, ask2_send, ask2_recv, hop1_send, hop1_recv, hop2_send, hop2_recv,
+    part_send, part_recv, whole_send, whole_recv, flag_send, flag_recv,
 ):
     t, c = lax.axis_index("tm"), lax.axis_index("chan")
-    y, z = c // 4, c % 4
+    first, second = (c // 4, c % 4), (c % 4, c // 4)
     windows, rows, length = raw.shape
-    groups = 16
+    side = 4
+    groups = side * side
     team = 8
     pair_count = out_ref.shape[0]
     share = pair_count // team
@@ -85,23 +88,20 @@
     for w in range(windows):
         load_copy(w).start()
 
-    def chan_peer(k):
-        return (y + k // 4) % 4 * 4 + (z + k % 4) % 4
-
-    def chan_from(k):
-        return (y + 4 - k // 4) % 4 * 4 + (z + 4 - k % 4) % 4
+    def chan_of(o, f, s):
+        return s * side + f if o else f * side + s
 
     barrier = pltpu.get_barrier_semaphore()
-
-    def greet_chan(k, _):
-        pl.semaphore_signal(barrier, inc=1, device_id=(t, chan_peer(k)), device_id_type=MESH)
-        return 0
+    for o in range(2):
+        for k in range(1, side):
+            pl.semaphore_signal(
+                barrier, inc=1, device_id=(t, chan_of(o, (first[o] + k) % side, second[o])), device_id_type=MESH
+            )
 
     def greet_tm(k, _):
         pl.semaphore_signal(barrier, inc=1, device_id=((t + k) % team, c), device_id_type=MESH)
         return 0
 
-    lax.fori_loop(1, groups, greet_chan, 0)
     lax.fori_loop(1, team, greet_tm, 0)
 
     small_copy(0).wait()
@@ -114,7 +114,8 @@
             one(low[e : e + 1] == place).astype(BF16), one(high[e : e + 1] == place).astype(BF16)
         )
     named = one(named > 0.0).astype(BF16)
-    marks_out[...] = jnp.zeros_like(marks_out)
+    marks[...] = jnp.zeros_like(marks)
+    recv2[...] = jnp.zeros_like(recv2)
     small_copy(1).wait()
 
     def mark(j, _):
@@ -123,32 +124,35 @@
         found = dot(named, one(ids // 128 == place).astype(BF16))
         line = jnp.sum(jnp.where(ids % 128 == place, found, 0.0), axis=0, keepdims=True)
         for k in range(10):
-            marks_out[j * 2 + k // 5, pl.ds(k % 5, 1), :] = line[:, k * 128 : (k + 1) * 128]
+            r = j * 2 + k // 5
+            bit = line[:, k * 128 : (k + 1) * 128]
+            marks[1, r, pl.ds(k % 5, 1), :] = bit
+            marks[0, r % side * side + r // side, pl.ds(k % 5, 1), :] = bit
         return 0
 
     lax.fori_loop(0, groups // 2, mark, 0)
-    marks = marks_out[...].reshape(128, 128)
-    ranks, before = ranks_of(marks)
-    own_rank[...] = jnp.where(ranks < CAP, ranks, -1.0)
-    sub = iota((128, 128), 0) % 8
-    over = jnp.max(jnp.where((sub == 5) & (before > CAP), 1.0, 0.0), axis=0, keepdims=True)
-    marks_out[...] = jnp.where(sub == 5, over, marks).reshape(groups, 8, 128)
-    marks_in[pl.ds(c, 1)] = marks_out[pl.ds(c, 1)]
-
-    pl.semaphore_wait(barrier, groups + team - 2)
-
-    def mark_copy(k):
-        p = chan_peer(k)
-        return pltpu.make_async_remote_copy(
-            marks_out.at[p], marks_in.at[c], mark_send.at[k], mark_recv.at[k],
-            device_id=(t, p), device_id_type=MESH,
-        )
-
-    def start_mark(k, _):
-        mark_copy(k).start()
-        return 0
-
-    lax.fori_loop(1, groups, start_mark, 0)
+
+    pl.semaphore_wait(barrier, 2 * (side - 1) + team - 1)
+
+    def ask1(o, k):
+        s = (second[o] + k) % side
+        return pltpu.make_async_remote_copy(
+            marks.at[o, pl.ds(s * side, side)], inner.at[o, second[o]], ask1_send.at[o, k], ask1_recv.at[o, k],
+            device_id=(t, chan_of(o, first[o], s)), device_id_type=MESH,
+        )
+
+    def ask2(o, k):
+        f = (first[o] + k) % side
+        return pltpu.make_async_remote_copy(
+            union.at[o, f], wanted.at[o, first[o]], ask2_send.at[o, k], ask2_recv.at[o, k],
+            device_id=(t, chan_of(o, f, second[o])), device_id_type=MESH,
+        )
+
+    for k in (2, 1, 3):
+        for o in range(2):
+            ask1(o, k).start()
+    for o in range(2):
+        inner[o, pl.ds(second[o], 1)] = marks[o, pl.ds(second[o] * side, side)][None]
 
     small_copy(2).wait()
     shifted = jnp.broadcast_to(
@@ -171,7 +175,7 @@
     band = one(near | (to_bin >= NB)).astype(BF16)
     lower = iota((rows // 2, NB), 1) < NB // 2
 
-    for w in range(windows):
+    def whiten(w):
         load_copy(w).wait()
         for half in range(2):
             here = pl.ds(half * (rows // 2), rows // 2)
@@ -187,66 +191,137 @@
             white[0, here, lanes] = jnp.where(lower, re, roll_half(im)).astype(BF16)
             white[1, here, lanes] = jnp.where(lower, roll_half(re), im).astype(BF16)
 
-    def end_mark(k, _):
-        mark_copy(k).wait_recv()
-        return 0
-
-    lax.fori_loop(1, groups, end_mark, 0)
-    asked = marks_in[...].reshape(128, 128)
-    flag_ref[0] = jnp.max(jnp.where(sub == 5, asked, 0.0))
-    rank[...] = ranks_of(asked)[0]
-
-    def row_copy(h, k):
-        p = chan_peer(k)
-        return pltpu.make_async_remote_copy(
-            send.at[h, p], recv.at[h, c], row_send.at[h, k], row_recv.at[h, k],
-            device_id=(t, p), device_id_type=MESH,
-        )
-
-    def ship(h):
-        for k in (8, 4, 12, 0):
-            picks = []
-            for m in range(4):
-                ranked = row_of(rank, chan_peer(k + m) * 8)
-                picks.append(one(ranked == iota((CAP, rows), 0).astype(F32)))
-            chosen = dot(jnp.concatenate(picks, axis=0).astype(BF16), white[h])
-            for m in range(4):
-                mine = chosen[m * CAP : (m + 1) * CAP]
-                send[h, pl.ds(chan_peer(k + m), 1)] = jnp.concatenate(
-                    [mine[:, : 2 * NB], mine[:, 2 * NB :]], axis=0
-                ).astype(BF16)[None]
-            for m in (2, 1, 3, 0):
-                if k + m:
-                    row_copy(h, k + m).start()
-
-    ship(0)
-    ship(1)
-
-    def name_slots(j, _):
-        found = jnp.zeros((8, 128), F32)
-        for h in range(2):
-            r = j * 2 + h
-            ids = row_of(rec, r * 5)
-            ranked = row_of(own_rank, r * 8)
-            spot = jnp.where(ranked >= 0.0, ranked + h * SLOT, -1.0)
-            chosen = one(spot == iota((128, rows), 0).astype(F32)).astype(BF16)
-            kind = iota((8, rows), 0)
-            values = jnp.where(
-                kind == 0, (ids // 128).astype(F32), jnp.where(kind == 1, (ids % 128).astype(F32), 1.0)
+    whiten(0)
+    whiten(1)
+    for o in range(2):
+        for k in range(1, side):
+            ask1(o, k).wait_recv()
+    for o in range(2):
+        either = inner[o, 0]
+        for ps in range(1, side):
+            either += inner[o, ps]
+        union[o] = one(either > 0.0)
+    for k in (2, 1, 3):
+        for o in range(2):
+            ask2(o, k).start()
+    for o in range(2):
+        wanted[o, pl.ds(first[o], 1)] = union[o, pl.ds(first[o], 1)]
+    whiten(2)
+    whiten(3)
+    ranks = ranks_of(inner[...].reshape(2 * groups * 8, 128), side * 8)
+    inner_rank[...] = ranks
+    over = jnp.max(one(ranks >= CAP2), axis=0, keepdims=True)
+    ranks = ranks_of(union[...].reshape(2 * side * 8, 128), 8)
+    union_rank[...] = ranks
+    over = jnp.maximum(over, jnp.max(one(ranks >= CAP1), axis=0, keepdims=True))
+    flags[0, 0] = jnp.broadcast_to(over, (8, 128))
+    for o in range(2):
+        for k in range(1, side):
+            ask2(o, k).wait_recv()
+    wanted_rank[...] = ranks_of(wanted[...].reshape(2 * side * 8, 128), 8)
+
+    def hop1(o, h, k):
+        f = (first[o] + k) % side
+        return pltpu.make_async_remote_copy(
+            send1.at[o, h, f], recv1.at[o, h, first[o]], hop1_send.at[o, h, k], hop1_recv.at[o, h, k],
+            device_id=(t, chan_of(o, f, second[o])), device_id_type=MESH,
+        )
+
+    def hop2(o, h, k):
+        s = (second[o] + k) % side
+        return pltpu.make_async_remote_copy(
+            send2.at[o, h, s], recv2.at[o, h, second[o], pl.ds(0, CAP2)], hop2_send.at[o, h, k], hop2_recv.at[o, h, k],
+            device_id=(t, chan_of(o, first[o], s)), device_id_type=MESH,
+        )
+
+    def flag_copy(o, k):
+        to = chan_of(o, (first[o] + k) % side, second[o])
+        return pltpu.make_async_remote_copy(
+            flags.at[o, 0], flags.at[o, k], flag_send.at[o, k], flag_recv.at[o, k],
+            device_id=(t, to), device_id_type=MESH,
+        )
+
+    for h in range(2):
+        for o in range(2):
+            if h == 0:
+                for pf in range(side):
+                    ranked = row_of(wanted_rank, o * side * 8 + pf * 8)
+                    pick1[o, pl.ds(pf * CAP1, CAP1), :] = one(
+                        ranked == iota((CAP1, rows), 0).astype(F32)
+                    ).astype(BF16)
+            lanes = pl.ds(o * 2 * NB, 2 * NB)
+            send1[o, h] = dot(pick1[o], white[h, :, lanes]).astype(BF16).reshape(side, CAP1, 2 * NB)
+            for k in (2, 1, 3):
+                hop1(o, h, k).start()
+            recv1[o, h, pl.ds(first[o], 1)] = send1[o, h, pl.ds(first[o], 1)]
+    for k in range(1, side):
+        flag_copy(0, k).start()
+
+    for o in range(2):
+
+        def cross_over(rf, _, o=o):
+            into = one(
+                row_of(union_rank, o * side * 8 + rf * 8) == iota((CAP1, rows), 0).astype(F32)
+            ).astype(BF16)
+            for ps in range(side):
+                out = one(
+                    row_of(inner_rank, o * groups * 8 + ps * side * 8 + rf * 8) == iota((CAP2, rows), 0).astype(F32)
+                ).astype(BF16)
+                pick2[o, rf, pl.ds(ps * CAP2, CAP2), :] = dot_nt(out, into).astype(BF16)
+            return 0
+
+        lax.fori_loop(0, side, cross_over, 0)
+
+    def forward(h):
+        for o in range(2):
+            for k in range(1, side):
+                hop1(o, h, k).wait_recv()
+            total = dot(pick2[o, 0], recv1[o, h, 0])
+            for rf in range(1, side):
+                total += dot(pick2[o, rf], recv1[o, h, rf])
+            send2[o, h] = total.astype(BF16).reshape(side, CAP2, 2 * NB)
+            for k in (2, 1, 3):
+                hop2(o, h, k).start()
+            recv2[o, h, pl.ds(second[o], 1), pl.ds(0, CAP2)] = send2[o, h, pl.ds(second[o], 1)]
+
+    forward(0)
+    ranks = ranks_of(marks[...].reshape(2 * groups * 8, 128), side * 8)
+    own_rank[...] = jnp.where(ranks < CAP2, ranks, -1.0)
+
+    columns = jnp.concatenate([ends.astype(F32), jnp.zeros((6, pair_count), F32)], axis=0).T
+
+    def name_slots(o):
+        def name_line(rs, _):
+            found = jnp.zeros((8, SLOT), F32)
+            for rf in range(side):
+                ids = row_of(rec, chan_of(o, rf, rs) * 5)
+                ranked = row_of(own_rank, o * groups * 8 + rs * side * 8 + rf * 8)
+                chosen = one(ranked == iota((SLOT, rows), 0).astype(F32)).astype(BF16)
+                kind = iota((8, rows), 0)
+                values = jnp.where(
+                    kind == 0, (ids // 128).astype(F32), jnp.where(kind == 1, (ids % 128).astype(F32), 1.0)
+                )
+                found += dot_nt(values.astype(BF16), chosen)
+            slot[pl.ds(o * side + rs, 1), :] = jnp.where(
+                found[2:3] > 0.0, found[0:1] * 128.0 + found[1:2], -1.0
             )
-            found += dot_nt(values.astype(BF16), chosen)
-        slot[pl.ds(j, 1), :] = jnp.where(
-            found[2:3] > 0.0, found[0:1] * 128.0 + found[1:2], -1.0
-        )
-        return 0
-
-    lax.fori_loop(0, groups // 2, name_slots, 0)
-    columns = jnp.concatenate([ends.astype(F32), jnp.zeros((6, pair_count), F32)], axis=0).T
-    for e in range(2):
-        for j in range(groups // 2):
-            take[e, :, j * 128 : (j + 1) * 128] = one(
-                columns[:, e : e + 1] == slot[j : j + 1, :]
-            ).astype(BF16)
+            return 0
+
+        lax.fori_loop(0, side, name_line, 0)
+        for e in range(2):
+            for rs in range(side):
+                take[o, e, :, rs * SLOT : (rs + 1) * SLOT] = one(
+                    columns[:, e : e + 1] == slot[o * side + rs : o * side + rs + 1, :]
+                ).astype(BF16)
+
+    name_slots(0)
+    forward(1)
+    name_slots(1)
+    for k in range(1, side):
+        flag_copy(0, k).wait_recv()
+    flags[1, 0] = jnp.max(flags[0], axis=0)
+    for k in range(1, side):
+        flag_copy(1, k).start()
 
     def part_copy(h, to, source):
         return pltpu.make_async_remote_copy(
@@ -259,16 +334,6 @@
             whole.at[h, t], whole.at[h, t], whole_send.at[h, k], whole_recv.at[h, k],
             device_id=((t + k) % team, c), device_id_type=MESH,
         )
-
-    def settle(h, r):
-        got = recv[h, pl.ds(r, 1)][0].astype(F32)
-        arrived[pl.ds(pl.multiple_of(r * SLOT, SLOT), SLOT), :] = jnp.concatenate(
-            [
-                jnp.concatenate([got[:CAP], got[CAP:]], axis=1),
-                jnp.zeros((SLOT - CAP, 4 * NB), F32),
-            ],
-            axis=0,
-        ).astype(BF16)
 
     def add_parts(h):
         def end_part(k, _):
@@ -285,27 +350,23 @@
         lax.fori_loop(1, team, start_whole, 0)
 
     for h in range(2):
-        recv[h, pl.ds(c, 1)] = send[h, pl.ds(c, 1)]
-        settle(h, c)
-
-        def end_row(k, _, h=h):
-            row_copy(h, k).wait_recv()
-            settle(h, chan_from(k))
-            return 0
-
-        lax.fori_loop(1, groups, end_row, 0)
+        for o in range(2):
+            for k in range(1, side):
+                hop2(o, h, k).wait_recv()
         if h:
             add_parts(0)
         for q in range(2):
             some = pl.ds(q * (pair_count // 2), pair_count // 2)
-            a = dot(take[0, some, :], arrived[...])
-            b = dot(take[1, some, :], arrived[...])
             straight = jnp.zeros((pair_count // 2, NB), F32)
             crossed = jnp.zeros((pair_count // 2, NB), F32)
-            for w in range(windows):
-                aw, bw = a[:, w * NB : (w + 1) * NB], b[:, w * NB : (w + 1) * NB]
-                straight += aw * bw
-                crossed += aw * roll_half(bw)
+            for o in range(2):
+                arrived = recv2[o, h].reshape(side * SLOT, 2 * NB)
+                a = dot(take[o, 0, some, :], arrived)
+                b = dot(take[o, 1, some, :], arrived)
+                for w in range(2):
+                    aw, bw = a[:, w * NB : (w + 1) * NB], b[:, w * NB : (w + 1) * NB]
+                    straight += aw * bw
+                    crossed += aw * roll_half(bw)
             lower = iota((pair_count // 2, NB), 1) < NB // 2
             product = jnp.where(lower, straight + roll_half(straight), crossed - roll_half(crossed))
             part[h, pl.ds(q * (team // 2), team // 2)] = (
@@ -328,17 +389,23 @@
         return 0
 
     lax.fori_loop(1, team, end_whole, 0)
-    first = whole[0].astype(F32).reshape(pair_count, NB)
-    second = whole[1].astype(F32).reshape(pair_count, NB)
+    near_bins = whole[0].astype(F32).reshape(pair_count, NB)
+    far_bins = whole[1].astype(F32).reshape(pair_count, NB)
     lower = iota((pair_count, NB), 1) < NB // 2
-    out_ref[:, :NB] = jnp.where(lower, first, roll_half(second)).astype(BF16)
-    out_ref[:, NB:] = jnp.where(lower, roll_half(first), second).astype(BF16)
-
-    def end_sends(k, _):
-        mark_copy(k).wait_send()
-        for h in range(2):
-            row_copy(h, k).wait_send()
-        return 0
+    out_ref[:, :NB] = jnp.where(lower, near_bins, roll_half(far_bins)).astype(BF16)
+    out_ref[:, NB:] = jnp.where(lower, roll_half(near_bins), far_bins).astype(BF16)
+    for k in range(1, side):
+        flag_copy(1, k).wait_recv()
+    flag_ref[0] = jnp.max(flags[1])
+
+    for o in range(2):
+        for k in range(1, side):
+            ask1(o, k).wait_send()
+            ask2(o, k).wait_send()
+            flag_copy(o, k).wait_send()
+            for h in range(2):
+                hop1(o, h, k).wait_send()
+                hop2(o, h, k).wait_send()
 
     def end_team_sends(k, _):
         for h in range(2):
@@ -346,7 +413,6 @@
             whole_copy(h, k).wait_send()
         return 0
 
-    lax.fori_loop(1, groups, end_sends, 0)
     lax.fori_loop(1, team, end_team_sends, 0)
 
 
@@ -391,7 +457,7 @@
 def local(raw_blocks, fir_taps, recorder_channel, pairs):
     windows, rows, length = raw_blocks.shape
     pair_count = pairs.shape[0]
-    groups, team = 16, 8
+    side, groups, team = 4, 16, 8
     share = pair_count // team
     table = jnp.asarray(table_values(length, 128))
     hbm = pl.BlockSpec(memory_space=pltpu.HBM)
@@ -413,28 +479,42 @@
             pltpu.VMEM((length + 128, 2 * NB), BF16),
             pltpu.VMEM((length, 2 * NB), BF16),
             pltpu.VMEM((2, rows, windows * NB), BF16),
-            pltpu.VMEM((groups, 8, 128), F32),
-            pltpu.VMEM((groups, 8, 128), F32),
-            pltpu.VMEM((groups * 8, 128), F32),
-            pltpu.VMEM((groups * 8, 128), F32),
-            pltpu.VMEM((2, groups, 2 * CAP, 2 * NB), BF16),
-            pltpu.VMEM((2, groups, 2 * CAP, 2 * NB), BF16),
-            pltpu.VMEM((groups * SLOT, windows * NB), BF16),
-            pltpu.VMEM((groups // 2, 128), F32),
-            pltpu.VMEM((2, pair_count, groups * SLOT), BF16),
+            pltpu.VMEM((2, groups, 8, 128), F32),
+            pltpu.VMEM((2, side, side, 8, 128), F32),
+            pltpu.VMEM((2, side, 8, 128), F32),
+            pltpu.VMEM((2, side, 8, 128), F32),
+            pltpu.VMEM((2 * groups * 8, 128), F32),
+            pltpu.VMEM((2 * groups * 8, 128), F32),
+            pltpu.VMEM((2 * side * 8, 128), F32),
+            pltpu.VMEM((2 * side * 8, 128), F32),
+            pltpu.VMEM((2, side * CAP1, rows), BF16),
+            pltpu.VMEM((2, side, side * CAP2, CAP1), BF16),
+            pltpu.VMEM((2, 2, side, CAP1, 2 * NB), BF16),
+            pltpu.VMEM((2, 2, side, CAP1, 2 * NB), BF16),
+            pltpu.VMEM((2, 2, side, CAP2, 2 * NB), BF16),
+            pltpu.VMEM((2, 2, side, SLOT, 2 * NB), BF16),
+            pltpu.VMEM((2 * side, SLOT), F32),
+            pltpu.VMEM((2, 2, pair_count, side * SLOT), BF16),
             pltpu.VMEM((2, team, share, NB), BF16),
             pltpu.VMEM((2, team, share, NB), BF16),
             pltpu.VMEM((2, team, share, NB), BF16),
+            pltpu.VMEM((2, side, 8, 128), F32),
             dma((windows,)),
             dma((4,)),
-            dma((groups,)),
-            dma((groups,)),
-            dma((2, groups)),
-            dma((2, groups)),
+            dma((2, side)),
+            dma((2, side)),
+            dma((2, side)),
+            dma((2, side)),
+            dma((2, 2, side)),
+            dma((2, 2, side)),
+            dma((2, 2, side)),
+            dma((2, 2, side)),
             dma((2, team)),
             dma((2, team)),
             dma((2, team)),
             dma((2, team)),
+            dma((2, side)),
+            dma((2, side)),
         ],
         compiler_params=pltpu.CompilerParams(
             collective_id=0, has_side_effects=True, vmem_limit_bytes=40 * 2**20

time: 51.8 us -> 51 us (0.985)
  Pallas kernels: 50.2 us -> 49.4 us
    pallas_call x1, Pallas kernels: 50.2 us -> 49.4 us  [local(): pl.pallas_call(kernel, out_shape=[jax.ShapeDtypeStruct((pair_count, 2 * N...]
where the time goes in v3:
time: 51 us; the launch traced here: 50.9 us
  Pallas kernels  49.4 us (97%)
  other arithmetic  0.83 us (2%)
  between operations  0.67 us (1%)
    pallas_call x1, Pallas kernels, local(): pl.pallas_call(kernel, out_shape=[jax.ShapeDtypeStruct((pair_count, 2 * N...  49.4 us

profile of v3, /device:TPU:1, one launch (start us, length us, event | category | flops | bytes accessed | tf_op | source)
XLA Modules:
  0.0 50.9 jit_solution(192634597725316609)
XLA Ops:
  0.0 0.0 copy-start
  0.0 0.0 copy-start.2
  0.0 0.0 copy-start.7
  0.0 49.4 %shard_map.57 = (bf16[512,256]{1,0:T(8,128)(2,1)S(1)}, f32[1]{0:T(128)}) custom-call(bf16[4,640,1024]{2,1,0:T(8,128)(2,1)} %raw_hbm.1, bf16[1,128]{1,0:T(2,128)(2,1)} %bitcast.23, s32[80,128]{1,0:T(8,128)} %bitcast.25, s32[2,512]{1,0:T(2,128)} %bitcast.30, bf16[1152,256]{1,0:T(8,128)(2,1)} %constant.98.clone.table_hbm), custom_call_target="tpu_custom_call" | custom-call | tf_op jit(solution)/shard_map/pallas_call | solution.py:466
  50.1 0.0 copy-done
  50.1 0.0 copy-done.2
  50.1 0.0 copy-done.7
  50.1 0.8 %conditional.1 = (f32[512,256]{1,0:T(8,128)}) conditional(s32[]{:T(128)} %bitcast.5, bf16[512,256]{1,0:T(8,128)(2,1)S(1)} %get-tuple-element.130, (bf16[128]{0:T(256)(128)(2,1)S(1)}, s32[10240]{0:T(1024)S(1)}, s32[512,2]{0,1:T(2,128)S(1)}, bf16[4,640,1024]{2,1,0:T(8,128)(2,1)}, bf16[1152,256]{1,0:T(8,128)(2,1)}) %tuple.62), branch_computations={%region_0.0_spmd, %region_1.10_spmd} | conditional | flops 1828508544 | bytes 94291416 | solution.py:523
  50.1 0.8 %convert_element_type.34 = f32[512,256]{1,0:T(8,128)} convert(bf16[512,256]{1,0:T(8,128)(2,1)S(1)} %param) | non-fusion elementwise | flops 131072 | bytes 786432 | tf_op jit(solution)/shard_map/cond/branch_0_fun/convert_element_type | solution.py:526
Async XLA Ops:
  0.0 50.1 %copy-start = (bf16[128]{0:T(256)(128)(2,1)S(1)}, bf16[128]{0:T(256)(128)(2,1)}, u32[]{:S(2)}) copy-start(bf16[128]{0:T(256)(128)(2,1)} %param.14) | copy-start | bytes 772
  0.0 50.1 %copy-start.2 = (s32[10240]{0:T(1024)S(1)}, s32[10240]{0:T(1024)}, u32[]{:S(2)}) copy-start(s32[10240]{0:T(1024)} %param.15) | copy-start | bytes 122884
  0.0 50.1 %copy-start.7 = (s32[512,2]{0,1:T(2,128)S(1)}, s32[512,2]{0,1:T(2,128)}, u32[]{:S(2)}) copy-start(s32[512,2]{0,1:T(2,128)} %param.16) | copy-start | bytes 12292

commit v4 on v3

--- a/solution.py
+++ b/solution.py
@@ -116,6 +116,7 @@
     named = one(named > 0.0).astype(BF16)
     marks[...] = jnp.zeros_like(marks)
     recv2[...] = jnp.zeros_like(recv2)
+    slot[...] = jnp.full_like(slot, -1.0)
     small_copy(1).wait()
 
     def mark(j, _):
@@ -193,6 +194,8 @@
 
     whiten(0)
     whiten(1)
+    owned = ranks_of(marks[...].reshape(2 * groups * 8, 128), side * 8)
+    own_rank[...] = jnp.where(owned < CAP2, owned, -1.0)
     for o in range(2):
         for k in range(1, side):
             ask1(o, k).wait_recv()
@@ -263,14 +266,40 @@
             into = one(
                 row_of(union_rank, o * side * 8 + rf * 8) == iota((CAP1, rows), 0).astype(F32)
             ).astype(BF16)
-            for ps in range(side):
-                out = one(
-                    row_of(inner_rank, o * groups * 8 + ps * side * 8 + rf * 8) == iota((CAP2, rows), 0).astype(F32)
+            out = [
+                one(row_of(inner_rank, o * groups * 8 + ps * side * 8 + rf * 8) == iota((CAP2, rows), 0).astype(F32))
+                for ps in range(side)
+            ]
+            pick2[o, pl.ds(rf, 1)] = dot_nt(jnp.concatenate(out, axis=0).astype(BF16), into).astype(BF16)[None]
+            return 0
+
+        lax.fori_loop(0, side, cross_over, 0)
+
+    columns = jnp.concatenate([ends.astype(F32), jnp.zeros((6, pair_count), F32)], axis=0).T
+
+    def name_slots(o):
+        def name_line(rs, _):
+            found = jnp.zeros((8, CAP2), F32)
+            for rf in range(side):
+                ids = row_of(rec, chan_of(o, rf, rs) * 5)
+                ranked = row_of(own_rank, o * groups * 8 + rs * side * 8 + rf * 8)
+                chosen = one(ranked == iota((CAP2, rows), 0).astype(F32)).astype(BF16)
+                kind = iota((8, rows), 0)
+                values = jnp.where(
+                    kind == 0, (ids // 128).astype(F32), jnp.where(kind == 1, (ids % 128).astype(F32), 1.0)
+                )
+                found += dot_nt(values.astype(BF16), chosen)
+            slot[pl.ds(o * side + rs, 1), pl.ds(0, CAP2)] = jnp.where(
+                found[2:3] > 0.0, found[0:1] * 128.0 + found[1:2], -1.0
+            )
+            return 0
+
+        lax.fori_loop(0, side, name_line, 0)
+        for e in range(2):
+            for rs in range(side):
+                take[o, e, :, rs * SLOT : (rs + 1) * SLOT] = one(
+                    columns[:, e : e + 1] == slot[o * side + rs : o * side + rs + 1, :]
                 ).astype(BF16)
-                pick2[o, rf, pl.ds(ps * CAP2, CAP2), :] = dot_nt(out, into).astype(BF16)
-            return 0
-
-        lax.fori_loop(0, side, cross_over, 0)
 
     def forward(h):
         for o in range(2):
@@ -285,35 +314,6 @@
             recv2[o, h, pl.ds(second[o], 1), pl.ds(0, CAP2)] = send2[o, h, pl.ds(second[o], 1)]
 
     forward(0)
-    ranks = ranks_of(marks[...].reshape(2 * groups * 8, 128), side * 8)
-    own_rank[...] = jnp.where(ranks < CAP2, ranks, -1.0)
-
-    columns = jnp.concatenate([ends.astype(F32), jnp.zeros((6, pair_count), F32)], axis=0).T
-
-    def name_slots(o):
-        def name_line(rs, _):
-            found = jnp.zeros((8, SLOT), F32)
-            for rf in range(side):
-                ids = row_of(rec, chan_of(o, rf, rs) * 5)
-                ranked = row_of(own_rank, o * groups * 8 + rs * side * 8 + rf * 8)
-                chosen = one(ranked == iota((SLOT, rows), 0).astype(F32)).astype(BF16)
-                kind = iota((8, rows), 0)
-                values = jnp.where(
-                    kind == 0, (ids // 128).astype(F32), jnp.where(kind == 1, (ids % 128).astype(F32), 1.0)
-                )
-                found += dot_nt(values.astype(BF16), chosen)
-            slot[pl.ds(o * side + rs, 1), :] = jnp.where(
-                found[2:3] > 0.0, found[0:1] * 128.0 + found[1:2], -1.0
-            )
-            return 0
-
-        lax.fori_loop(0, side, name_line, 0)
-        for e in range(2):
-            for rs in range(side):
-                take[o, e, :, rs * SLOT : (rs + 1) * SLOT] = one(
-                    columns[:, e : e + 1] == slot[o * side + rs : o * side + rs + 1, :]
-                ).astype(BF16)
-
     name_slots(0)
     forward(1)
     name_slots(1)
@@ -353,8 +353,6 @@
         for o in range(2):
             for k in range(1, side):
                 hop2(o, h, k).wait_recv()
-        if h:
-            add_parts(0)
         for q in range(2):
             some = pl.ds(q * (pair_count // 2), pair_count // 2)
             straight = jnp.zeros((pair_count // 2, NB), F32)
@@ -381,6 +379,7 @@
                 return 0
 
             lax.fori_loop(q * (team // 2), (q + 1) * (team // 2), start_part, 0)
+    add_parts(0)
     add_parts(1)
 
     def end_whole(k, _):

time: 51 us -> 48.2 us (0.945)
  Pallas kernels: 49.4 us -> 46.6 us
    pallas_call x1, Pallas kernels: 49.4 us -> 46.6 us  [local(): pl.pallas_call(kernel, out_shape=[jax.ShapeDtypeStruct((pair_count, 2 * N...]
where the time goes in v4:
time: 48.2 us; the launch traced here: 48.1 us
  Pallas kernels  46.6 us (97%)
  other arithmetic  0.83 us (2%)
  between operations  0.67 us (1%)
    pallas_call x1, Pallas kernels, local(): pl.pallas_call(kernel, out_shape=[jax.ShapeDtypeStruct((pair_count, 2 * N...  46.6 us

profile of v4, /device:TPU:1, one launch (start us, length us, event | category | flops | bytes accessed | tf_op | source)
XLA Modules:
  0.0 48.1 jit_solution(12941103411539130223)
XLA Ops:
  0.0 0.0 copy-start
  0.0 0.0 copy-start.2
  0.0 0.0 copy-start.7
  0.0 46.6 %shard_map.57 = (bf16[512,256]{1,0:T(8,128)(2,1)S(1)}, f32[1]{0:T(128)}) custom-call(bf16[4,640,1024]{2,1,0:T(8,128)(2,1)} %raw_hbm.1, bf16[1,128]{1,0:T(2,128)(2,1)} %bitcast.23, s32[80,128]{1,0:T(8,128)} %bitcast.25, s32[2,512]{1,0:T(2,128)} %bitcast.30, bf16[1152,256]{1,0:T(8,128)(2,1)} %constant.98.clone.table_hbm), custom_call_target="tpu_custom_call" | custom-call | tf_op jit(solution)/shard_map/pallas_call | solution.py:465
  47.2 0.0 copy-done
  47.2 0.0 copy-done.2
  47.2 0.0 copy-done.7
  47.2 0.8 %conditional.1 = (f32[512,256]{1,0:T(8,128)}) conditional(s32[]{:T(128)} %bitcast.5, bf16[512,256]{1,0:T(8,128)(2,1)S(1)} %get-tuple-element.130, (bf16[128]{0:T(256)(128)(2,1)S(1)}, s32[10240]{0:T(1024)S(1)}, s32[512,2]{0,1:T(2,128)S(1)}, bf16[4,640,1024]{2,1,0:T(8,128)(2,1)}, bf16[1152,256]{1,0:T(8,128)(2,1)}) %tuple.62), branch_computations={%region_0.0_spmd, %region_1.10_spmd} | conditional | flops 1828508544 | bytes 94291416 | solution.py:522
  47.2 0.8 %convert_element_type.34 = f32[512,256]{1,0:T(8,128)} convert(bf16[512,256]{1,0:T(8,128)(2,1)S(1)} %param) | non-fusion elementwise | flops 131072 | bytes 786432 | tf_op jit(solution)/shard_map/cond/branch_0_fun/convert_element_type | solution.py:525
Async XLA Ops:
  0.0 47.2 %copy-start = (bf16[128]{0:T(256)(128)(2,1)S(1)}, bf16[128]{0:T(256)(128)(2,1)}, u32[]{:S(2)}) copy-start(bf16[128]{0:T(256)(128)(2,1)} %param.14) | copy-start | bytes 772
  0.0 47.2 %copy-start.2 = (s32[10240]{0:T(1024)S(1)}, s32[10240]{0:T(1024)}, u32[]{:S(2)}) copy-start(s32[10240]{0:T(1024)} %param.15) | copy-start | bytes 122884
  0.0 47.2 %copy-start.7 = (s32[512,2]{0,1:T(2,128)S(1)}, s32[512,2]{0,1:T(2,128)}, u32[]{:S(2)}) copy-start(s32[512,2]{0,1:T(2,128)} %param.16) | copy-start | bytes 12292

commit v5 on v4

--- a/solution.py
+++ b/solution.py
@@ -115,8 +115,6 @@
         )
     named = one(named > 0.0).astype(BF16)
     marks[...] = jnp.zeros_like(marks)
-    recv2[...] = jnp.zeros_like(recv2)
-    slot[...] = jnp.full_like(slot, -1.0)
     small_copy(1).wait()
 
     def mark(j, _):
@@ -131,7 +129,7 @@
             marks[0, r % side * side + r // side, pl.ds(k % 5, 1), :] = bit
         return 0
 
-    lax.fori_loop(0, groups // 2, mark, 0)
+    lax.fori_loop(0, groups // 2, mark, 0, unroll=8)
 
     pl.semaphore_wait(barrier, 2 * (side - 1) + team - 1)
 
@@ -152,6 +150,8 @@
     for k in (2, 1, 3):
         for o in range(2):
             ask1(o, k).start()
+    recv2[:, :, :, CAP2:, :] = jnp.zeros((2, 2, side, SLOT - CAP2, 2 * NB), BF16)
+    slot[...] = jnp.full_like(slot, -1.0)
     for o in range(2):
         inner[o, pl.ds(second[o], 1)] = marks[o, pl.ds(second[o] * side, side)][None]
 
@@ -340,14 +340,11 @@
             part_copy(h, 0, (t + k) % team).wait_recv()
             return 0
 
-        def start_whole(k, _):
-            whole_copy(h, k).start()
-            return 0
-
         parts[h, pl.ds(t, 1)] = part[h, pl.ds(t, 1)]
         lax.fori_loop(1, team, end_part, 0)
         whole[h, pl.ds(t, 1)] = jnp.sum(parts[h].astype(F32), axis=0, keepdims=True).astype(BF16)
-        lax.fori_loop(1, team, start_whole, 0)
+        for k in (4, 5, 3, 2, 6, 7, 1):
+            whole_copy(h, k).start()
 
     for h in range(2):
         for o in range(2):

time: 48.2 us -> 47.2 us (0.979)
  Pallas kernels: 46.6 us -> 45.6 us
    pallas_call x1, Pallas kernels: 46.6 us -> 45.6 us  [local(): pl.pallas_call(kernel, out_shape=[jax.ShapeDtypeStruct((pair_count, 2 * N...]
where the time goes in v5:
time: 47.2 us; the launch traced here: 47.1 us
  Pallas kernels  45.6 us (97%)
  other arithmetic  0.83 us (2%)
  between operations  0.67 us (1%)
    pallas_call x1, Pallas kernels, local(): pl.pallas_call(kernel, out_shape=[jax.ShapeDtypeStruct((pair_count, 2 * N...  45.6 us

profile of v5, /device:TPU:1, one launch (start us, length us, event | category | flops | bytes accessed | tf_op | source)
XLA Modules:
  0.0 47.1 jit_solution(9673214865634487320)
XLA Ops:
  0.0 0.0 copy-start
  0.0 0.0 copy-start.2
  0.0 0.0 copy-start.7
  0.0 45.6 %shard_map.57 = (bf16[512,256]{1,0:T(8,128)(2,1)S(1)}, f32[1]{0:T(128)}) custom-call(bf16[4,640,1024]{2,1,0:T(8,128)(2,1)} %raw_hbm.1, bf16[1,128]{1,0:T(2,128)(2,1)} %bitcast.23, s32[80,128]{1,0:T(8,128)} %bitcast.25, s32[2,512]{1,0:T(2,128)} %bitcast.30, bf16[1152,256]{1,0:T(8,128)(2,1)} %constant.98.clone.table_hbm), custom_call_target="tpu_custom_call" | custom-call | tf_op jit(solution)/shard_map/pallas_call | solution.py:462
  46.3 0.0 copy-done
  46.3 0.0 copy-done.2
  46.3 0.0 copy-done.7
  46.3 0.8 %conditional.1 = (f32[512,256]{1,0:T(8,128)}) conditional(s32[]{:T(128)} %bitcast.5, bf16[512,256]{1,0:T(8,128)(2,1)S(1)} %get-tuple-element.130, (bf16[128]{0:T(256)(128)(2,1)S(1)}, s32[10240]{0:T(1024)S(1)}, s32[512,2]{0,1:T(2,128)S(1)}, bf16[4,640,1024]{2,1,0:T(8,128)(2,1)}, bf16[1152,256]{1,0:T(8,128)(2,1)}) %tuple.62), branch_computations={%region_0.0_spmd, %region_1.10_spmd} | conditional | flops 1828508544 | bytes 94291416 | solution.py:519
  46.3 0.8 %convert_element_type.34 = f32[512,256]{1,0:T(8,128)} convert(bf16[512,256]{1,0:T(8,128)(2,1)S(1)} %param) | non-fusion elementwise | flops 131072 | bytes 786432 | tf_op jit(solution)/shard_map/cond/branch_0_fun/convert_element_type | solution.py:522
Async XLA Ops:
  0.0 46.3 %copy-start = (bf16[128]{0:T(256)(128)(2,1)S(1)}, bf16[128]{0:T(256)(128)(2,1)}, u32[]{:S(2)}) copy-start(bf16[128]{0:T(256)(128)(2,1)} %param.14) | copy-start | bytes 772
  0.0 46.3 %copy-start.2 = (s32[10240]{0:T(1024)S(1)}, s32[10240]{0:T(1024)}, u32[]{:S(2)}) copy-start(s32[10240]{0:T(1024)} %param.15) | copy-start | bytes 122884
  0.0 46.3 %copy-start.7 = (s32[512,2]{0,1:T(2,128)S(1)}, s32[512,2]{0,1:T(2,128)}, u32[]{:S(2)}) copy-start(s32[512,2]{0,1:T(2,128)} %param.16) | copy-start | bytes 12292
